TPU v7x, 512 devices: a whole 4x8x8 slice. The times are simulated.
512 devices in a mesh: dp: 32 (over x, z), hid: 16 (over y, core).
Axes of the slice: x: 4, y: 8, z: 8, core: 2. Of those that a mesh axis runs over, the one named last changes fastest.
Arguments:
- inputs: bfloat16 [8192, 8192], P('dp', 'hid'), may hold values from -6 to 6
- out_grad: bfloat16 [8192, 8192], P('dp', 'hid'), may hold values from -6 to 6
- home_block: int32 [64], P('hid'), may hold values from 0 to 1
- blocks_up: bfloat16 [64, 3, 256, 256], P('hid', None, 'dp'), may hold values from -0.21875 to 0.21875
- blocks_down: bfloat16 [64, 3, 256, 256], P('hid', None, 'dp'), may hold values from -0.15625 to 0.15625
- up_left: bfloat16 [8192, 128], P('hid', 'dp'), may hold values from -0.0625 to 0.0625
- up_right: bfloat16 [128, 16384], P('dp', 'hid'), may hold values from -0.5 to 0.5
- down_left: bfloat16 [16384, 128], P('hid', 'dp'), may hold values from -0.046875 to 0.046875
- down_right: bfloat16 [128, 8192], P('dp', 'hid'), may hold values from -0.5 to 0.5
Outputs:
- outputs: bfloat16 [8192, 8192], P('dp', 'hid')
- input_grad: bfloat16 [8192, 8192], P('dp', 'hid')
- grad_blocks_up: bfloat16 [64, 3, 256, 256], P('hid', None, 'dp')
- grad_blocks_down: bfloat16 [64, 3, 256, 256], P('hid', None, 'dp')
- grad_up_left: bfloat16 [8192, 128], P('hid', 'dp')
- grad_up_right: bfloat16 [128, 16384], P('dp', 'hid')
- grad_down_left: bfloat16 [16384, 128], P('hid', 'dp')
- grad_down_right: bfloat16 [128, 8192], P('dp', 'hid')
All inputs are finite; a program needn't handle non-finite values.
Results may differ from a plain program's by a relative error of at most 0.022.
Values may be sent and summed in bfloat16 or wider, within the bound.
A program may use at most 64 MiB of HBM per device.

v0:
```python
import jax
import jax.numpy as jnp
from jax import lax
from jax.sharding import PartitionSpec as P

gelu_coef = 0.7978845608028654
cubic_coef = 0.044715


def from_partner(value, axis, distance):
    mask = 2**distance
    pairs = [(source, source ^ mask) for source in range(lax.axis_size(axis))]
    return lax.ppermute(value, axis, pairs)


def gelu_pair(pre_act):
    tangent = jnp.tanh(gelu_coef * (pre_act + cubic_coef * pre_act * pre_act * pre_act))
    activated = 0.5 * pre_act * (1.0 + tangent)
    derivative = 0.5 * (1.0 + tangent) + 0.5 * pre_act * (1.0 - tangent * tangent) * gelu_coef * (
        1.0 + 3.0 * cubic_coef * pre_act * pre_act
    )
    return (activated, derivative)


def per_device(
    inputs, out_grad, home_block, blocks_up, blocks_down, up_left, up_right, down_left, down_right
):
    single = jnp.float32
    half_type = jnp.bfloat16
    highest = lax.Precision.HIGHEST
    row_count, width_dev = inputs.shape
    hid_blocks, slot_count, shard_rows, blk_size = blocks_up.shape
    level_count = slot_count - 1
    in_blocks = width_dev // blk_size
    hidden_dev = hid_blocks * blk_size
    top_bit = lax.axis_size("hid").bit_length() - 1
    grad_scale = float(lax.axis_size("dp") * row_count) ** (-0.5)
    select = (home_block[:, None] == jnp.arange(in_blocks, dtype=jnp.int32)[None, :]).astype(single)
    full_up, full_down, left_in, right_in, left_out, right_out = (
        lax.all_gather(blocks_up, "dp", axis=2, tiled=True),
        lax.all_gather(blocks_down, "dp", axis=2, tiled=True),
        lax.all_gather(up_left, "dp", axis=1, tiled=True),
        lax.all_gather(up_right, "dp", axis=0, tiled=True),
        lax.all_gather(down_left, "dp", axis=1, tiled=True),
        lax.all_gather(down_right, "dp", axis=0, tiled=True),
    )
    rank_in = lax.psum(jnp.dot(inputs, left_in, preferred_element_type=single), "hid")
    rank_in = rank_in.astype(half_type)
    in_pieces = [inputs]
    grad_pieces = [out_grad]
    for level_idx in range(level_count):
        in_pieces.append(from_partner(inputs, "hid", top_bit - 1 - level_idx))

    def pick_blocks(pieces):
        stacked = jnp.stack(pieces, 0).reshape(slot_count, row_count, in_blocks, blk_size)
        return jnp.take(stacked, home_block, axis=2)

    picked = pick_blocks(in_pieces)
    part_rows = picked
    up_sum = jnp.einsum("sthk,hskn->thn", part_rows, full_up, preferred_element_type=single)
    pre_act = up_sum.reshape(row_count, hidden_dev) + jnp.dot(
        rank_in, right_in, preferred_element_type=single
    )
    activated, derivative = gelu_pair(pre_act)
    hidden = activated.astype(half_type)
    hidden_blocks = hidden.reshape(row_count, hid_blocks, blk_size)
    rank_mid = lax.psum(jnp.dot(hidden, left_out, preferred_element_type=single), "hid").astype(
        half_type
    )
    part_rows = hidden_blocks
    down_sum = jnp.einsum("thk,hskn->sthn", part_rows, full_down, preferred_element_type=single)
    placed = jnp.einsum("sthn,hi->stin", down_sum, select, precision=highest)
    total = placed[0]
    for level_idx in range(level_count):
        arrived = from_partner(placed[level_idx + 1], "hid", top_bit - 1 - level_idx)
        total = total + arrived
    outputs = (
        total.reshape(row_count, width_dev)
        + jnp.dot(rank_mid, right_out, preferred_element_type=single)
    ).astype(half_type)
    rank_back = lax.psum(jnp.dot(out_grad, right_out.T, preferred_element_type=single), "hid")
    rank_back = rank_back.astype(half_type)
    for level_idx in range(level_count):
        grad_pieces.append(from_partner(out_grad, "hid", top_bit - 1 - level_idx))
    grad_picked = pick_blocks(grad_pieces)
    grad_hidden = jnp.einsum(
        "sthn,hskn->thk", grad_picked, full_down, preferred_element_type=single
    )
    grad_pre = (
        (
            grad_hidden.reshape(row_count, hidden_dev)
            + jnp.dot(rank_back, left_out.T, preferred_element_type=single)
        )
        * derivative
    ).astype(half_type)
    rank_grad = lax.psum(
        jnp.dot(grad_pre, right_in.T, preferred_element_type=single), "hid"
    ).astype(half_type)
    grad_blocks = grad_pre.reshape(row_count, hid_blocks, blk_size)
    back_sum = jnp.einsum("thn,hskn->sthk", grad_blocks, full_up, preferred_element_type=single)
    back_placed = jnp.einsum("sthk,hi->stik", back_sum, select, precision=highest)
    back_total = back_placed[0]
    for level_idx in range(level_count):
        arrived = from_partner(back_placed[level_idx + 1], "hid", top_bit - 1 - level_idx)
        back_total = back_total + arrived
    input_grad = (
        back_total.reshape(row_count, width_dev)
        + jnp.dot(rank_grad, left_in.T, preferred_element_type=single)
    ).astype(half_type)
    summed = (
        lax.psum_scatter(
            (
                grad_scale
                * jnp.einsum("sthk,thn->hskn", picked, grad_blocks, preferred_element_type=single)
            ).astype(jnp.bfloat16),
            "dp",
            scatter_dimension=2,
            tiled=True,
        ).astype(jnp.float32),
        lax.psum_scatter(
            (
                grad_scale
                * jnp.einsum(
                    "thk,sthn->hskn", hidden_blocks, grad_picked, preferred_element_type=single
                )
            ).astype(jnp.bfloat16),
            "dp",
            scatter_dimension=2,
            tiled=True,
        ).astype(jnp.float32),
        lax.psum_scatter(
            (grad_scale * jnp.dot(inputs.T, rank_grad, preferred_element_type=single)).astype(
                jnp.bfloat16
            ),
            "dp",
            scatter_dimension=1,
            tiled=True,
        ).astype(jnp.float32),
        lax.psum_scatter(
            (grad_scale * jnp.dot(rank_in.T, grad_pre, preferred_element_type=single)).astype(
                jnp.bfloat16
            ),
            "dp",
            scatter_dimension=0,
            tiled=True,
        ).astype(jnp.float32),
        lax.psum_scatter(
            (grad_scale * jnp.dot(hidden.T, rank_back, preferred_element_type=single)).astype(
                jnp.bfloat16
            ),
            "dp",
            scatter_dimension=1,
            tiled=True,
        ).astype(jnp.float32),
        lax.psum_scatter(
            (grad_scale * jnp.dot(rank_mid.T, out_grad, preferred_element_type=single)).astype(
                jnp.bfloat16
            ),
            "dp",
            scatter_dimension=0,
            tiled=True,
        ).astype(jnp.float32),
    )
    return (outputs, input_grad) + tuple((summed_part.astype(half_type) for summed_part in summed))


def solution(mesh):
    placed = (
        P("dp", "hid"),
        P("dp", "hid"),
        P("hid"),
        P("hid", None, "dp", None),
        P("hid", None, "dp", None),
        P("hid", "dp"),
        P("dp", "hid"),
        P("hid", "dp"),
        P("dp", "hid"),
    )
    return jax.shard_map(
        per_device,
        mesh=mesh,
        in_specs=placed,
        out_specs=(
            P("dp", "hid"),
            P("dp", "hid"),
            P("hid", None, "dp", None),
            P("hid", None, "dp", None),
            P("hid", "dp"),
            P("dp", "hid"),
            P("hid", "dp"),
            P("dp", "hid"),
        ),
        check_vma=False,
    )
```

profile of v0, /device:TPU:8, one launch (start us, length us, event | category | flops | bytes accessed | tf_op | source)
XLA Modules:
  0.0 738.6 jit_solution(1994460682840392459)
XLA Ops:
  7.3 0.7 all-gather.7.cloned.1.call-update
  8.0 0.7 all-gather.9.cloned.1.call-update
  8.7 1.1 copy.54
  9.8 6.8 collective-permute-start
  16.7 2.7 collective-permute-start.1
  19.4 1.1 copy.63
  20.5 4.7 collective-permute-start.4
  25.2 2.2 collective-permute-start.5
  27.6 49.3 %all-gather = bf16[32,4,512]{2,1,0:T(4,128)(2,1)S(1)} all-gather(bf16[1,4,512]{2,1,0:T(4,128)(2,1)S(1)} %bitcast.138), channel_id=1, replica_groups=mesh['dp'=32,'hid'=16] {'dp'}, dimensions={0}, use_global_device_ids=true | all-gather | bytes 135168 | tf_op jit(solution)/shard_map/all_gather | solution.py:42
  77.2 42.4 %all-gather.3 = bf16[32,4,512]{2,1,0:T(4,128)(2,1)S(1)} all-gather(bf16[1,4,512]{2,1,0:T(4,128)(2,1)S(1)} %bitcast.139), channel_id=1, replica_groups=mesh['dp'=32,'hid'=16] {'dp'}, dimensions={0}, use_global_device_ids=true | all-gather | bytes 135168 | tf_op jit(solution)/shard_map/all_gather | solution.py:45
  119.9 46.7 %all-gather.1 = bf16[32,4,1024]{2,1,0:T(4,128)(2,1)S(1)} all-gather(bf16[1,4,1024]{2,1,0:T(4,128)(2,1)S(1)} %bitcast.136), channel_id=1, replica_groups=mesh['dp'=32,'hid'=16] {'dp'}, dimensions={0}, use_global_device_ids=true | all-gather | bytes 270336 | tf_op jit(solution)/shard_map/all_gather | solution.py:43
  166.7 0.8 copy.66
  167.6 45.5 %all-reduce.13 = (bf16[256,128]{1,0:T(8,128)(2,1)S(1)}, bf16[256,128]{1,0:T(8,128)(2,1)S(1)}) all-reduce(f32[256,128]{1,0:T(8,128)S(1)} %fusion.57, f32[256,128]{1,0:T(8,128)S(1)} %fusion.59), channel_id=1, replica_groups=mesh['dp'=32,'hid'=16] {'hid'}, use_global_device_ids=true, to_apply=%region_0.2 | all-reduce | flops 65536 | bytes 393216 | tf_op jit(solution)/shard_map/psum | solution.py:47
  213.1 48.1 %all-gather.2 = bf16[32,4,1024]{2,1,0:T(4,128)(2,1)S(1)} all-gather(bf16[1,4,1024]{2,1,0:T(4,128)(2,1)S(1)} %bitcast.137), channel_id=1, replica_groups=mesh['dp'=32,'hid'=16] {'dp'}, dimensions={0}, use_global_device_ids=true | all-gather | bytes 270336 | tf_op jit(solution)/shard_map/all_gather | solution.py:44
  261.2 0.8 reshape.83
  262.3 0.8 copy.67
  263.1 0.8 copy.68
  264.1 0.6 gather_fusion
  264.7 1.8 pad_maximum_fusion.1
  266.5 1.9 gather_fusion.1
  268.4 3.2 fusion.8
  271.6 2.6 copy.60
  274.2 3.1 fusion.5
  277.4 2.7 copy.89
  280.1 0.5 multiply_convert_fusion.2
  280.6 0.4 copy-done.7
  281.0 0.4 copy-done.9
  281.4 0.8 fusion.20
  282.5 1.0 fusion.21
  283.8 0.4 reshape.55
  284.1 1.0 fusion.22
  285.1 48.0 %all-reduce.14 = (bf16[256,128]{1,0:T(8,128)(2,1)S(1)}, bf16[256,128]{1,0:T(8,128)(2,1)S(1)}) all-reduce(f32[256,128]{1,0:T(8,128)S(1)} %fusion.58, f32[256,128]{1,0:T(8,128)S(1)} %fusion.60), channel_id=1, replica_groups=mesh['dp'=32,'hid'=16] {'hid'}, use_global_device_ids=true, to_apply=%region_1.0 | all-reduce | flops 65536 | bytes 393216 | tf_op jit(solution)/shard_map/psum | solution.py:67
  333.1 0.9 fusion.24
  334.0 0.9 fusion.25
  334.8 2.3 fusion.10
  337.1 2.4 copy.76
  339.7 1.4 dynamic-slice
  342.4 0.4 reshape.58
  342.8 0.9 multiply_convert_fusion.1
  343.7 1.4 copy.117
  345.0 2.9 reshape.97
  347.9 1.4 copy-done.3
  349.3 0.6 convolution_bitcast_fusion
  349.9 4.1 fusion.16
  354.0 0.4 slice_bitcast_fusion.1
  354.4 7.7 %collective-permute-start.6 = (f32[256,2,256]{2,1,0:T(2,128)S(1)}, f32[256,2,256]{2,1,0:T(2,128)S(1)}, u32[]{:S(2)}, u32[]{:S(2)}) collective-permute-start(f32[256,2,256]{2,1,0:T(2,128)S(1)} %get-tuple-element.50), channel_id=1, source_target_pairs={{0,8},{1,9},{2,10},{3,11},{4,12},{5,13},{6,14},{7,15},{8,0},{9,1},... | collective-permute-start | bytes 1572872 | tf_op jit(solution)/shard_map/ppermute | solution.py:13
  362.1 1.9 collective-permute-start.7
  364.0 0.6 convolution_bitcast_fusion.1
  364.6 4.1 fusion.13
  369.1 7.0 collective-permute-start.2
  376.1 1.9 collective-permute-start.3
  378.4 62.6 %collective-permute-done.7 = f32[256,2,256]{2,1,0:T(2,128)S(1)} collective-permute-done((f32[256,2,256]{2,1,0:T(2,128)S(1)}, f32[256,2,256]{2,1,0:T(2,128)S(1)}, u32[]{:S(2)}, u32[]{:S(2)}) %collective-permute-start.7) | collective-permute-done | bytes 524320 | tf_op jit(solution)/shard_map/ppermute | solution.py:13
  441.4 10.7 %collective-permute-done.3 = f32[256,2,256]{2,1,0:T(2,128)S(1)} collective-permute-done((f32[256,2,256]{2,1,0:T(2,128)S(1)}, f32[256,2,256]{2,1,0:T(2,128)S(1)}, u32[]{:S(2)}, u32[]{:S(2)}) %collective-permute-start.3) | collective-permute-done | bytes 524320 | tf_op jit(solution)/shard_map/ppermute | solution.py:13
  452.5 0.9 add_convert_fusion
  453.5 52.5 %all-reduce.12.cloned.1.call-done = (bf16[4,3,256,256]{3,0,1,2:T(4,128)(2,1)}, bf16[512,128]{0,1:T(8,128)(2,1)}, bf16[128,1024]{1,0:T(8,128)(2,1)}, bf16[1024,128]{0,1:T(8,128)(2,1)}, bf16[128,512]{1,0:T(8,128)(2,1)}) async-done(((bf16[4,3,256,256]{3,0,1,2:T(4,128)(2,1)}, bf16[512,128]{0,1:T(8,128)(2,1)}, bf16[128,1024]{1,0:T(8,128)(2,1)}, bf16[1024,128]{0,1:T(8,128)(2,1)}, bf16[128,512]{1,0:T(8,128)(2,1)}), ...) | async-done | bytes 2359312
  505.9 0.8 constant_dynamic-slice_fusion.4
  506.7 0.6 copy.77
  507.4 1.3 constant_dynamic-slice_fusion
  508.7 1.3 constant_dynamic-slice_fusion.3
  510.0 1.3 constant_dynamic-slice_fusion.1
  511.3 1.3 constant_dynamic-slice_fusion.2
  512.6 218.0 %reduce-scatter.4.cloned.1.call-done = bf16[8,3072]{1,0:T(8,128)(2,1)} async-done(((bf16[256,3072]{1,0:T(8,128)(2,1)}), bf16[8,3072]{1,0:T(8,128)(2,1)}) %reduce-scatter.4.cloned.1.call-update) | async-done | bytes 49168
  730.6 0.9 reshape.98
  731.5 0.6 copy.97
  (62 shorter events, 3.7 us)
Async XLA Ops:
  7.2 69.8 %copy-start.2 = (bf16[256,512]{1,0:T(8,128)(2,1)S(1)}, bf16[256,512]{1,0:T(8,128)(2,1)}, u32[]{:S(2)}) copy-start(bf16[256,512]{1,0:T(8,128)(2,1)} %param.11) | copy-start | bytes 786436
  7.2 112.5 %copy-start.1 = (bf16[256,512]{1,0:T(8,128)(2,1)S(1)}, bf16[256,512]{1,0:T(8,128)(2,1)}, u32[]{:S(2)}) copy-start(bf16[256,512]{1,0:T(8,128)(2,1)} %param.12) | copy-start | bytes 786436
  7.2 20.4 %copy-start.12 = (bf16[512,4]{0,1:T(4,128)(2,1)S(1)}, bf16[512,4]{0,1:T(4,128)(2,1)}, u32[]{:S(2)}) copy-start(bf16[512,4]{0,1:T(4,128)(2,1)} %param.16) | copy-start | bytes 12292
  7.2 70.0 %copy-start.13 = (bf16[4,512]{1,0:T(4,128)(2,1)S(1)}, bf16[4,512]{1,0:T(4,128)(2,1)}, u32[]{:S(2)}) copy-start(bf16[4,512]{1,0:T(4,128)(2,1)} %param.19) | copy-start | bytes 12292
  7.2 261.2 %all-gather.7.cloned.1.call-start = ((), (), s32[]{:S(2)}) async-start(), calls=%async_computation.1 | async-start | bytes 1622016 | tf_op jit(solution)/shard_map/all_gather | solution.py:40
  7.9 266.3 %all-gather.9.cloned.1.call-start = ((), (), s32[]{:S(2)}) async-start(), calls=%async_computation.2 | async-start | bytes 1622016 | tf_op jit(solution)/shard_map/all_gather | solution.py:41
  8.7 497.2 %all-reduce.12.cloned.1.call-start = ((), (), s32[]{:S(2)}) async-start(), calls=%async_computation.4 | async-start | bytes 4718592
  9.8 110.1 %copy-start.10 = (bf16[4,1024]{1,0:T(4,128)(2,1)S(1)}, bf16[4,1024]{1,0:T(4,128)(2,1)}, u32[]{:S(2)}) copy-start(bf16[4,1024]{1,0:T(4,128)(2,1)} %param.17) | copy-start | bytes 24580
  9.8 252.2 %collective-permute-start = (bf16[256,512]{0,1:T(8,128)(2,1)S(1)}, bf16[256,512]{0,1:T(8,128)(2,1)S(1)}, u32[]{:S(2)}, u32[]{:S(2)}) collective-permute-start(bf16[256,512]{0,1:T(8,128)(2,1)S(1)} %copy.54), channel_id=1, source_target_pairs={{0,8},{1,9},{2,10},{3,11},{4,12},{5,13},{6,14},{7,15},{8,0},{9,1},... | collective-permute-start | bytes 786440 | tf_op jit(solution)/shard_map/ppermute | solution.py:13
  16.7 245.5 %collective-permute-start.1 = (bf16[256,512]{0,1:T(8,128)(2,1)S(1)}, bf16[256,512]{0,1:T(8,128)(2,1)S(1)}, u32[]{:S(2)}, u32[]{:S(2)}) collective-permute-start(bf16[256,512]{0,1:T(8,128)(2,1)S(1)} %copy.54), channel_id=1, source_target_pairs={{0,4},{1,5},{2,6},{3,7},{4,0},{5,1},{6,2},{7,3},{8,12},{9,13},{10,... | collective-permute-start | bytes 786440 | tf_op jit(solution)/shard_map/ppermute | solution.py:13
  20.5 241.8 %collective-permute-start.4 = (bf16[256,512]{0,1:T(8,128)(2,1)S(1)}, bf16[256,512]{0,1:T(8,128)(2,1)S(1)}, u32[]{:S(2)}, u32[]{:S(2)}) collective-permute-start(bf16[256,512]{0,1:T(8,128)(2,1)S(1)} %copy.63), channel_id=1, source_target_pairs={{0,8},{1,9},{2,10},{3,11},{4,12},{5,13},{6,14},{7,15},{8,0},{9,1},... | collective-permute-start | bytes 786440 | tf_op jit(solution)/shard_map/ppermute | solution.py:13
  25.2 237.9 %collective-permute-start.5 = (bf16[256,512]{0,1:T(8,128)(2,1)S(1)}, bf16[256,512]{0,1:T(8,128)(2,1)S(1)}, u32[]{:S(2)}, u32[]{:S(2)}) collective-permute-start(bf16[256,512]{0,1:T(8,128)(2,1)S(1)} %copy.63), channel_id=1, source_target_pairs={{0,4},{1,5},{2,6},{3,7},{4,0},{5,1},{6,2},{7,3},{8,12},{9,13},{10,... | collective-permute-start | bytes 786440 | tf_op jit(solution)/shard_map/ppermute | solution.py:13
  27.6 139.9 %copy-start.14 = (s32[4]{0:T(128)S(1)}, s32[4]{0:T(128)}, u32[]{:S(2)}) copy-start(s32[4]{0:T(128)} %param.13) | copy-start | bytes 52
  77.0 136.1 %copy-start.11 = (bf16[1024,4]{0,1:T(4,128)(2,1)S(1)}, bf16[1024,4]{0,1:T(4,128)(2,1)}, u32[]{:S(2)}) copy-start(bf16[1024,4]{0,1:T(4,128)(2,1)} %param.18) | copy-start | bytes 24580
  264.7 3.6 copy-start.4
  271.6 2.7 copy-start.6
  277.4 2.7 copy-start.8
  280.1 0.9 copy-start.7
  280.1 1.3 copy-start.9
  339.5 3.3 copy-start.5
  339.5 391.1 %reduce-scatter.4.cloned.1.call-start = ((), (), s32[]{:S(2)}) async-start(), calls=%async_computation.3 | async-start | bytes 1622016
  347.9 1.4 copy-start.3
  354.0 10.0 %copy-start = (bf16[4,3,256,256]{3,2,1,0:T(8,128)(2,1)S(1)}, bf16[4,3,256,256]{3,2,1,0:T(8,128)(2,1)}, u32[]{:S(2)}) copy-start(bf16[4,3,256,256]{3,2,1,0:T(8,128)(2,1)} %all-gather.9.cloned.1.call-done) | copy-start | bytes 4718596
  354.4 24.0 %collective-permute-start.6 = (f32[256,2,256]{2,1,0:T(2,128)S(1)}, f32[256,2,256]{2,1,0:T(2,128)S(1)}, u32[]{:S(2)}, u32[]{:S(2)}) collective-permute-start(f32[256,2,256]{2,1,0:T(2,128)S(1)} %get-tuple-element.50), channel_id=1, source_target_pairs={{0,8},{1,9},{2,10},{3,11},{4,12},{5,13},{6,14},{7,15},{8,0},{9,1},... | collective-permute-start | bytes 1572872 | tf_op jit(solution)/shard_map/ppermute | solution.py:13
  362.1 78.9 %collective-permute-start.7 = (f32[256,2,256]{2,1,0:T(2,128)S(1)}, f32[256,2,256]{2,1,0:T(2,128)S(1)}, u32[]{:S(2)}, u32[]{:S(2)}) collective-permute-start(f32[256,2,256]{2,1,0:T(2,128)S(1)} %get-tuple-element.51), channel_id=1, source_target_pairs={{0,4},{1,5},{2,6},{3,7},{4,0},{5,1},{6,2},{7,3},{8,12},{9,13},{10,... | collective-permute-start | bytes 1572872 | tf_op jit(solution)/shard_map/ppermute | solution.py:13
  369.1 72.3 %collective-permute-start.2 = (f32[256,2,256]{2,1,0:T(2,128)S(1)}, f32[256,2,256]{2,1,0:T(2,128)S(1)}, u32[]{:S(2)}, u32[]{:S(2)}) collective-permute-start(f32[256,2,256]{2,1,0:T(2,128)S(1)} %get-tuple-element.52), channel_id=1, source_target_pairs={{0,8},{1,9},{2,10},{3,11},{4,12},{5,13},{6,14},{7,15},{8,0},{9,1},... | collective-permute-start | bytes 1572872 | tf_op jit(solution)/shard_map/ppermute | solution.py:13
  376.1 76.1 %collective-permute-start.3 = (f32[256,2,256]{2,1,0:T(2,128)S(1)}, f32[256,2,256]{2,1,0:T(2,128)S(1)}, u32[]{:S(2)}, u32[]{:S(2)}) collective-permute-start(f32[256,2,256]{2,1,0:T(2,128)S(1)} %get-tuple-element.53), channel_id=1, source_target_pairs={{0,4},{1,5},{2,6},{3,7},{4,0},{5,1},{6,2},{7,3},{8,12},{9,13},{10,... | collective-permute-start | bytes 1572872 | tf_op jit(solution)/shard_map/ppermute | solution.py:13
Sparse Core Ops, SparseCore 0:
  11.1 83.7 all-gather.6
  97.9 77.6 all-gather.8
  339.6 166.2 all-reduce.11
  510.8 219.7 reduce-scatter.3
where the time goes:
time: 740 us; the launch traced here: 739 us
  waiting for transfers between devices  345 us (47%)
  blocking collectives  280 us (38%)
  starting transfers between devices  35.3 us (5%)
  local copies, waits for them, and re-layouts  33.8 us (5%)
  matrix products  25.2 us (3%)
  between operations  15.6 us (2%)
    unnamed x6, waiting for transfers between devices  272 us
    ppermute x8, waiting for transfers between devices, from_partner(): return lax.ppermute(value, axis, pairs)  73.3 us
    all_gather x1, blocking collectives, per_device(): lax.all_gather(up_left, 'dp', axis=1, tiled=True)  49.3 us
    all_gather x1, blocking collectives, per_device(): lax.all_gather(down_left, 'dp', axis=1, tiled=True)  48.1 us
    psum x1, blocking collectives, per_device(): lax.psum(jnp.dot(hidden, left_out, preferred_element_type=single), 'hid')  48 us
    all_gather x1, blocking collectives, per_device(): lax.all_gather(up_right, 'dp', axis=0, tiled=True)  46.7 us
    psum x1, blocking collectives, per_device(): lax.psum(jnp.dot(inputs, left_in, preferred_element_type=single), 'hid')  45.5 us
    all_gather x1, blocking collectives, per_device(): lax.all_gather(down_right, 'dp', axis=0, tiled=True)  42.4 us
  transfers between devices with their start and end apart: 12, of which 4 were waited for; matrix products, arithmetic and copies ran while one was open for 6% of the time, Pallas kernels for 0%

commit v1 on v0

--- a/solution.py
+++ b/solution.py
@@ -64,9 +64,9 @@
     activated, derivative = gelu_pair(pre_act)
     hidden = activated.astype(half_type)
     hidden_blocks = hidden.reshape(row_count, hid_blocks, blk_size)
-    rank_mid = lax.psum(jnp.dot(hidden, left_out, preferred_element_type=single), "hid").astype(
-        half_type
-    )
+    rank_mid = jnp.sum(
+        lax.all_gather(jnp.dot(hidden, left_out, preferred_element_type=single), "hid"), axis=0
+    ).astype(half_type)
     part_rows = hidden_blocks
     down_sum = jnp.einsum("thk,hskn->sthn", part_rows, full_down, preferred_element_type=single)
     placed = jnp.einsum("sthn,hi->stin", down_sum, select, precision=highest)

time: 740 us -> 716 us (0.968)
  waiting for transfers between devices: 345 us -> 295 us
  blocking collectives: 280 us -> 294 us
  matrix products: 25.2 us -> 33.5 us
    unnamed x6 -> x7, waiting for transfers between devices: 272 us -> 245 us
    ppermute x8, waiting for transfers between devices: 73.3 us -> 50 us  [from_partner(): return lax.ppermute(value, axis, pairs)]
    psum x1, blocking collectives: 48 us -> 60.6 us  [per_device(): lax.psum(jnp.dot(grad_pre, right_in.T, preferred_element_type=single), 'h...]
    unnamed x49 -> x71, local copies, waits for them, and re-layouts: 19.2 us -> 17.5 us
  transfers between devices with their start and end apart: 12 -> 13, of which waited for: 4 -> 6; matrix products, arithmetic and copies ran while one was open for 6% -> 9% of each run, Pallas kernels for 0% -> 0%
where the time goes in v1:
time: 716 us; the launch traced here: 715 us
  waiting for transfers between devices  295 us (41%)
  blocking collectives  294 us (41%)
  starting transfers between devices  38.4 us (5%)
  matrix products  33.5 us (5%)
  local copies, waits for them, and re-layouts  31 us (4%)
  between operations  15.7 us (2%)
  other arithmetic  7.23 us (1%)
    unnamed x7, waiting for transfers between devices  245 us
    psum x1, blocking collectives, per_device(): lax.psum(jnp.dot(grad_pre, right_in.T, preferred_element_type=single), 'h...  60.6 us
    ppermute x8, waiting for transfers between devices, from_partner(): return lax.ppermute(value, axis, pairs)  50 us
    all_gather x1, blocking collectives, per_device(): lax.all_gather(up_left, 'dp', axis=1, tiled=True)  49.3 us
    all_gather x1, blocking collectives, per_device(): lax.all_gather(down_left, 'dp', axis=1, tiled=True)  48.4 us
    all_gather x1, blocking collectives, per_device(): lax.all_gather(up_right, 'dp', axis=0, tiled=True)  46.6 us
    psum x1, blocking collectives, per_device(): lax.psum(jnp.dot(inputs, left_in, preferred_element_type=single), 'hid')  46.6 us
    all_gather x1, blocking collectives, per_device(): lax.all_gather(down_right, 'dp', axis=0, tiled=True)  42.4 us
  transfers between devices with their start and end apart: 13, of which 6 were waited for; matrix products, arithmetic and copies ran while one was open for 9% of the time, Pallas kernels for 0%

profile of v1, /device:TPU:8, one launch (start us, length us, event | category | flops | bytes accessed | tf_op | source)
XLA Modules:
  0.0 714.9 jit_solution(11925692941078519738)
XLA Ops:
  7.3 0.7 all-gather.9.cloned.1.call-update
  8.0 0.7 all-gather.11.cloned.1.call-update
  8.7 1.1 copy.54
  9.8 6.8 collective-permute-start
  16.7 2.7 collective-permute-start.1
  19.5 49.3 %all-gather.1 = bf16[32,4,512]{2,1,0:T(4,128)(2,1)S(1)} all-gather(bf16[1,4,512]{2,1,0:T(4,128)(2,1)} %bitcast.140), channel_id=1, replica_groups=mesh['dp'=32,'hid'=16] {'dp'}, dimensions={0}, use_global_device_ids=true | all-gather | bytes 135168 | tf_op jit(solution)/shard_map/all_gather | solution.py:42
  69.2 42.4 %all-gather.4 = bf16[32,4,512]{2,1,0:T(4,128)(2,1)S(1)} all-gather(bf16[1,4,512]{2,1,0:T(4,128)(2,1)S(1)} %bitcast.141), channel_id=1, replica_groups=mesh['dp'=32,'hid'=16] {'dp'}, dimensions={0}, use_global_device_ids=true | all-gather | bytes 135168 | tf_op jit(solution)/shard_map/all_gather | solution.py:45
  111.8 46.6 %all-gather.2 = bf16[32,4,1024]{2,1,0:T(4,128)(2,1)S(1)} all-gather(bf16[1,4,1024]{2,1,0:T(4,128)(2,1)S(1)} %bitcast.138), channel_id=1, replica_groups=mesh['dp'=32,'hid'=16] {'dp'}, dimensions={0}, use_global_device_ids=true | all-gather | bytes 270336 | tf_op jit(solution)/shard_map/all_gather | solution.py:43
  158.5 0.8 reshape.82
  159.2 46.6 %all-reduce.12 = (bf16[256,128]{1,0:T(8,128)(2,1)}, bf16[256,128]{1,0:T(8,128)(2,1)}) all-reduce(f32[256,128]{1,0:T(8,128)S(1)} %fusion.57, f32[256,128]{1,0:T(8,128)S(1)} %fusion.59), channel_id=1, replica_groups=mesh['dp'=32,'hid'=16] {'hid'}, use_global_device_ids=true, to_apply=%region_0.2 | all-reduce | flops 65536 | bytes 393216 | tf_op jit(solution)/shard_map/psum | solution.py:47
  205.8 48.4 %all-gather.3 = bf16[32,4,1024]{2,1,0:T(4,128)(2,1)S(1)} all-gather(bf16[1,4,1024]{2,1,0:T(4,128)(2,1)S(1)} %bitcast.139), channel_id=1, replica_groups=mesh['dp'=32,'hid'=16] {'dp'}, dimensions={0}, use_global_device_ids=true | all-gather | bytes 270336 | tf_op jit(solution)/shard_map/all_gather | solution.py:44
  254.2 0.8 reshape.84
  255.4 0.6 gather_fusion
  256.1 3.7 fusion.8
  259.8 1.6 copy.60
  261.4 1.5 multiply_convert_fusion.2
  262.9 1.0 fusion.58
  264.1 4.0 collective-permute-start.4
  268.1 4.9 collective-permute-start.5
  273.2 4.2 collective-permute-done.4
  277.6 7.9 %collective-permute-done.5 = bf16[256,512]{0,1:T(8,128)(2,1)S(1)} collective-permute-done((bf16[256,512]{0,1:T(8,128)(2,1)S(1)}, bf16[256,512]{0,1:T(8,128)(2,1)S(1)}, u32[]{:S(2)}, u32[]{:S(2)}) %collective-permute-start.5) | collective-permute-done | bytes 262176 | tf_op jit(solution)/shard_map/ppermute | solution.py:13
  285.7 1.8 gather_fusion.1
  287.6 2.6 fusion.5
  290.2 1.3 copy.89
  291.5 2.5 fusion.20
  294.4 0.8 copy-done.5
  295.2 0.9 multiply_convert_fusion.1
  296.0 1.4 copy.117
  297.4 2.9 reshape.98
  301.0 2.1 fusion.60
  303.1 2.0 fusion.10
  305.1 3.8 copy.76
  308.9 2.0 convolution_bitcast_fusion
  311.0 4.1 fusion.16
  315.1 1.4 slice_bitcast_fusion.1
  316.5 5.2 collective-permute-start.6
  321.7 5.3 collective-permute-start.7
  327.0 60.6 %all-reduce.13 = bf16[256,128]{1,0:T(8,128)(2,1)S(1)} all-reduce(f32[256,128]{1,0:T(8,128)S(1)} %copy-done.18), channel_id=1, replica_groups=mesh['dp'=32,'hid'=16] {'hid'}, use_global_device_ids=true, to_apply=%region_3.5 | all-reduce | flops 32768 | bytes 196608 | tf_op jit(solution)/shard_map/psum | solution.py:96
  387.7 0.9 fusion.25
  388.6 1.0 fusion.21
  389.5 1.0 fusion.22
  390.5 2.3 reduce_sum.9
  392.9 1.8 fusion.24
  394.7 1.6 convolution_bitcast_fusion.1
  396.3 4.1 fusion.13
  400.4 1.3 slice_bitcast_fusion.4
  401.8 5.0 collective-permute-start.2
  406.8 3.9 collective-permute-start.3
  410.8 1.3 dynamic-slice
  413.6 1.6 fusion.32
  415.2 6.5 collective-permute-done.2
  421.7 31.3 %collective-permute-done.3 = f32[256,2,256]{2,1,0:T(2,128)} collective-permute-done((f32[256,2,256]{2,1,0:T(2,128)}, f32[256,2,256]{2,1,0:T(2,128)}, u32[]{:S(2)}, u32[]{:S(2)}) %collective-permute-start.3) | collective-permute-done | bytes 524320 | tf_op jit(solution)/shard_map/ppermute | solution.py:13
  453.0 1.6 fusion.34
  454.6 0.8 add_convert_fusion
  455.4 77.0 %reduce-scatter.4.cloned.1.call-done = bf16[8,3072]{1,0:T(8,128)(2,1)} async-done(((bf16[256,3072]{1,0:T(8,128)(2,1)}), bf16[8,3072]{1,0:T(8,128)(2,1)}) %reduce-scatter.4.cloned.1.call-update) | async-done | bytes 49168
  532.4 0.9 reshape.99
  533.3 0.6 copy.97
  534.1 0.8 add_convert_fusion.1
  534.9 166.8 %all-reduce.11.cloned.1.call-done = (bf16[4,3,256,256]{3,0,1,2:T(4,128)(2,1)}, bf16[512,128]{0,1:T(8,128)(2,1)}, bf16[128,1024]{1,0:T(8,128)(2,1)}, bf16[1024,128]{0,1:T(8,128)(2,1)}, bf16[128,512]{1,0:T(8,128)(2,1)}) async-done(((bf16[4,3,256,256]{3,0,1,2:T(4,128)(2,1)}, bf16[512,128]{0,1:T(8,128)(2,1)}, bf16[128,1024]{1,0:T(8,128)(2,1)}, bf16[1024,128]{0,1:T(8,128)(2,1)}, bf16[128,512]{1,0:T(8,128)(2,1)}), ...) | async-done | bytes 2359312
  701.7 0.8 constant_dynamic-slice_fusion.4
  703.1 1.3 constant_dynamic-slice_fusion.1
  704.4 1.3 constant_dynamic-slice_fusion.2
  705.8 1.3 constant_dynamic-slice_fusion
  707.1 1.3 constant_dynamic-slice_fusion.3
  (89 shorter events, 4.1 us)
Async XLA Ops:
  7.2 61.7 %copy-start.2 = (bf16[256,512]{1,0:T(8,128)(2,1)S(1)}, bf16[256,512]{1,0:T(8,128)(2,1)}, u32[]{:S(2)}) copy-start(bf16[256,512]{1,0:T(8,128)(2,1)} %param.11) | copy-start | bytes 786436
  7.2 62.0 %copy-start.24 = (bf16[4,512]{1,0:T(4,128)(2,1)S(1)}, bf16[4,512]{1,0:T(4,128)(2,1)}, u32[]{:S(2)}) copy-start(bf16[4,512]{1,0:T(4,128)(2,1)} %param.19) | copy-start | bytes 12292
  7.2 104.4 %copy-start.3 = (bf16[256,512]{1,0:T(8,128)(2,1)S(1)}, bf16[256,512]{1,0:T(8,128)(2,1)}, u32[]{:S(2)}) copy-start(bf16[256,512]{1,0:T(8,128)(2,1)} %param.12) | copy-start | bytes 786436
  7.2 104.6 %copy-start.22 = (bf16[4,1024]{1,0:T(4,128)(2,1)S(1)}, bf16[4,1024]{1,0:T(4,128)(2,1)}, u32[]{:S(2)}) copy-start(bf16[4,1024]{1,0:T(4,128)(2,1)} %param.17) | copy-start | bytes 24580
  7.2 248.9 %all-gather.9.cloned.1.call-start = ((), (), s32[]{:S(2)}) async-start(), calls=%async_computation.1 | async-start | bytes 1622016 | tf_op jit(solution)/shard_map/all_gather | solution.py:40
  7.9 279.6 %all-gather.11.cloned.1.call-start = ((), (), s32[]{:S(2)}) async-start(), calls=%async_computation.2 | async-start | bytes 1622016 | tf_op jit(solution)/shard_map/all_gather | solution.py:41
  8.7 381.8 %all-gather.13.cloned.1.call-start = ((), (), s32[]{:S(2)}) async-start(), calls=%async_computation.3 | async-start | bytes 2228224 | tf_op jit(solution)/shard_map/all_gather | solution.py:68
  9.8 245.2 %collective-permute-start = (bf16[256,512]{0,1:T(8,128)(2,1)S(1)}, bf16[256,512]{0,1:T(8,128)(2,1)S(1)}, u32[]{:S(2)}, u32[]{:S(2)}) collective-permute-start(bf16[256,512]{0,1:T(8,128)(2,1)S(1)} %copy.54), channel_id=1, source_target_pairs={{0,8},{1,9},{2,10},{3,11},{4,12},{5,13},{6,14},{7,15},{8,0},{9,1},... | collective-permute-start | bytes 786440 | tf_op jit(solution)/shard_map/ppermute | solution.py:13
  16.7 238.5 %collective-permute-start.1 = (bf16[256,512]{0,1:T(8,128)(2,1)S(1)}, bf16[256,512]{0,1:T(8,128)(2,1)S(1)}, u32[]{:S(2)}, u32[]{:S(2)}) collective-permute-start(bf16[256,512]{0,1:T(8,128)(2,1)S(1)} %copy.54), channel_id=1, source_target_pairs={{0,4},{1,5},{2,6},{3,7},{4,0},{5,1},{6,2},{7,3},{8,12},{9,13},{10,... | collective-permute-start | bytes 786440 | tf_op jit(solution)/shard_map/ppermute | solution.py:13
  19.4 139.9 %copy-start.25 = (s32[4]{0:T(128)S(1)}, s32[4]{0:T(128)}, u32[]{:S(2)}) copy-start(s32[4]{0:T(128)} %param.13) | copy-start | bytes 52
  19.5 186.3 %copy-start.23 = (bf16[1024,4]{0,1:T(4,128)(2,1)S(1)}, bf16[1024,4]{0,1:T(4,128)(2,1)}, u32[]{:S(2)}) copy-start(bf16[1024,4]{0,1:T(4,128)(2,1)} %param.18) | copy-start | bytes 24580
  68.9 186.1 %copy-start.10 = (bf16[128,512]{1,0:T(8,128)(2,1)}, bf16[128,512]{1,0:T(8,128)(2,1)S(1)}, u32[]{:S(2)}) copy-start(bf16[128,512]{1,0:T(8,128)(2,1)S(1)} %reshape.80) | copy-start | bytes 393220
  256.1 3.7 copy-start.7
  259.8 1.6 copy-start.12
  259.8 1.6 copy-start.20
  261.4 1.5 copy-start.13
  263.9 268.5 %reduce-scatter.4.cloned.1.call-start = ((), (), s32[]{:S(2)}) async-start(), calls=%async_computation.4 | async-start | bytes 1622016
  264.1 13.3 %collective-permute-start.4 = (bf16[256,512]{0,1:T(8,128)(2,1)S(1)}, bf16[256,512]{0,1:T(8,128)(2,1)S(1)}, u32[]{:S(2)}, u32[]{:S(2)}) collective-permute-start(bf16[256,512]{0,1:T(8,128)(2,1)S(1)} %copy.63), channel_id=1, source_target_pairs={{0,8},{1,9},{2,10},{3,11},{4,12},{5,13},{6,14},{7,15},{8,0},{9,1},... | collective-permute-start | bytes 786440 | tf_op jit(solution)/shard_map/ppermute | solution.py:13
  268.1 17.4 %collective-permute-start.5 = (bf16[256,512]{0,1:T(8,128)(2,1)S(1)}, bf16[256,512]{0,1:T(8,128)(2,1)S(1)}, u32[]{:S(2)}, u32[]{:S(2)}) collective-permute-start(bf16[256,512]{0,1:T(8,128)(2,1)S(1)} %copy.63), channel_id=1, source_target_pairs={{0,4},{1,5},{2,6},{3,7},{4,0},{5,1},{6,2},{7,3},{8,12},{9,13},{10,... | collective-permute-start | bytes 786440 | tf_op jit(solution)/shard_map/ppermute | solution.py:13
  290.2 1.3 copy-start.14
  291.5 3.6 copy-start.8
  294.4 0.8 copy-start.5
  300.3 2.8 copy-start.9
  300.3 401.3 %all-reduce.11.cloned.1.call-start = ((), (), s32[]{:S(2)}) async-start(), calls=%async_computation.5 | async-start | bytes 4718592
  301.0 8.0 %copy-start.1 = (bf16[256,4,256]{2,1,0:T(4,128)(2,1)}, bf16[256,4,256]{2,1,0:T(4,128)(2,1)S(1)}, u32[]{:S(2)}) copy-start(bf16[256,4,256]{2,1,0:T(4,128)(2,1)S(1)} %reshape.55) | copy-start | bytes 1572868
  305.1 3.9 copy-start.6
  315.1 12.0 %copy-start.18 = (f32[256,128]{1,0:T(8,128)S(1)}, f32[256,128]{1,0:T(8,128)}, u32[]{:S(2)}) copy-start(f32[256,128]{1,0:T(8,128)} %fusion.60) | copy-start | bytes 393220
  315.1 73.5 %copy-start.21 = (bf16[256,128]{1,0:T(8,128)(2,1)S(1)}, bf16[256,128]{1,0:T(8,128)(2,1)}, u32[]{:S(2)}) copy-start(bf16[256,128]{1,0:T(8,128)(2,1)} %get-tuple-element.41) | copy-start | bytes 196612
  315.1 74.4 %copy-start.19 = (bf16[256,128]{1,0:T(8,128)(2,1)S(1)}, bf16[256,128]{1,0:T(8,128)(2,1)}, u32[]{:S(2)}) copy-start(bf16[256,128]{1,0:T(8,128)(2,1)} %get-tuple-element.42) | copy-start | bytes 196612
  316.5 97.1 %collective-permute-start.6 = (f32[256,2,256]{2,1,0:T(2,128)}, f32[256,2,256]{2,1,0:T(2,128)}, u32[]{:S(2)}, u32[]{:S(2)}) collective-permute-start(f32[256,2,256]{2,1,0:T(2,128)} %get-tuple-element.48), channel_id=1, source_target_pairs={{0,8},{1,9},{2,10},{3,11},{4,12},{5,13},{6,14},{7,15},{8,0},{9,1},... | collective-permute-start | bytes 1572872 | tf_op jit(solution)/shard_map/ppermute | solution.py:13
  321.7 91.9 %collective-permute-start.7 = (f32[256,2,256]{2,1,0:T(2,128)}, f32[256,2,256]{2,1,0:T(2,128)}, u32[]{:S(2)}, u32[]{:S(2)}) collective-permute-start(f32[256,2,256]{2,1,0:T(2,128)} %get-tuple-element.49), channel_id=1, source_target_pairs={{0,4},{1,5},{2,6},{3,7},{4,0},{5,1},{6,2},{7,3},{8,12},{9,13},{10,... | collective-permute-start | bytes 1572872 | tf_op jit(solution)/shard_map/ppermute | solution.py:13
  387.7 2.8 copy-start.16
  389.5 3.3 copy-start.4
  392.8 1.9 copy-start
  400.4 12.9 %copy-start.11 = (bf16[128,512]{1,0:T(8,128)(2,1)S(1)}, bf16[128,512]{1,0:T(8,128)(2,1)}, u32[]{:S(2)}) copy-start(bf16[128,512]{1,0:T(8,128)(2,1)} %copy-done.10) | copy-start | bytes 393220
  400.4 12.9 %copy-start.17 = (bf16[256,128]{1,0:T(8,128)(2,1)S(1)}, bf16[256,128]{1,0:T(8,128)(2,1)}, u32[]{:S(2)}) copy-start(bf16[256,128]{1,0:T(8,128)(2,1)} %copy-done.16) | copy-start | bytes 196612
  401.8 19.9 %collective-permute-start.2 = (f32[256,2,256]{2,1,0:T(2,128)}, f32[256,2,256]{2,1,0:T(2,128)}, u32[]{:S(2)}, u32[]{:S(2)}) collective-permute-start(f32[256,2,256]{2,1,0:T(2,128)} %get-tuple-element.50), channel_id=1, source_target_pairs={{0,8},{1,9},{2,10},{3,11},{4,12},{5,13},{6,14},{7,15},{8,0},{9,1},... | collective-permute-start | bytes 1572872 | tf_op jit(solution)/shard_map/ppermute | solution.py:13
  406.8 46.2 %collective-permute-start.3 = (f32[256,2,256]{2,1,0:T(2,128)}, f32[256,2,256]{2,1,0:T(2,128)}, u32[]{:S(2)}, u32[]{:S(2)}) collective-permute-start(f32[256,2,256]{2,1,0:T(2,128)} %get-tuple-element.51), channel_id=1, source_target_pairs={{0,4},{1,5},{2,6},{3,7},{4,0},{5,1},{6,2},{7,3},{8,12},{9,13},{10,... | collective-permute-start | bytes 1572872 | tf_op jit(solution)/shard_map/ppermute | solution.py:13
  454.6 79.3 %copy-start.15 = (bf16[256,128]{1,0:T(8,128)(2,1)S(1)}, bf16[256,128]{1,0:T(8,128)(2,1)}, u32[]{:S(2)}) copy-start(bf16[256,128]{1,0:T(8,128)(2,1)} %reduce_sum.9) | copy-start | bytes 196612
Sparse Core Ops, SparseCore 0:
  11.1 83.6 all-gather.8
  97.8 77.9 all-gather.10
  264.0 39.6 all-gather.12
  308.1 224.2 reduce-scatter.3
  536.3 165.3 all-reduce.10
